TPU v7x, 256 devices: a whole 4x4x8 slice. The times are simulated.
256 devices in a mesh: wide: 64 (over y, x_lo, z), lev: 4 (over x_hi, core).
Axes of the slice: x: 4 (x_hi: 2, x_lo: 2; x = x_hi * 2 + x_lo), y: 4, z: 8, core: 2. Of those that a mesh axis runs over, the one named last changes fastest.
Arguments:
- state_field: float32 [12, 1472, 1472], P('lev', 'wide'), may hold values from -8 to 8
- to_modes: float32 [12, 12], replicated, may hold values from -4 to 4
- from_modes: float32 [12, 12], replicated, may hold values from -4 to 4, as said below
- mode_depth: float32 [12], replicated, may hold values from 0.1 to 2000
Outputs:
- updated_field: float32 [12, 1472, 1472], P('lev', 'wide')
Inputs may be any that keep to these rules, and one draw needn't show every extreme that they name: `from_modes`: the inverse of to_modes.
All inputs are finite; a program needn't handle non-finite values.
Results may differ from a plain program's by a relative error of at most 0.000094.
Values sent between devices are 32-bit elements; how exact they have to be, the bound alone decides.
A program may use at most 64 MiB of HBM per device.

v0:
```python
import math

import jax
import jax.numpy as jnp
from jax import lax
from jax.sharding import PartitionSpec as P

I = 1472
E = 64
KT = 512


highest = lax.Precision.HIGHEST


def spread(block, axis, owner):
    block = jnp.where(lax.axis_index(axis) == owner, block, jnp.zeros_like(block))
    return lax.psum(block, axis)


def blend_weights(fraction):
    square = fraction * fraction
    cubed = square * fraction
    return (
        2.0 * cubed - 3.0 * square + 1.0,
        cubed - 2.0 * square + fraction,
        -2.0 * cubed + 3.0 * square,
        cubed - square,
    )


def hermite_mix(start_val, start_slope, end_val, end_slope, weights):
    return (
        weights[0] * end_val
        + weights[1] * end_slope
        + weights[2] * start_val
        + weights[3] * start_slope
    )


def extend_cols(sub_block, extra):
    fraction = (jnp.arange(extra, dtype=jnp.float32) + 1.0) / (extra + 1.0)
    weights = blend_weights(fraction)
    end_val = sub_block[..., -1:]
    end_slope = sub_block[..., -1:] - sub_block[..., -2:-1]
    start_val = sub_block[..., :1]
    start_slope = sub_block[..., 1:2] - sub_block[..., :1]
    added = hermite_mix(start_val, start_slope, end_val, end_slope, weights)
    return jnp.concatenate([sub_block, added], axis=-1)


def laplace(waves, length):
    sines = jnp.sin(math.pi / length * waves.astype(jnp.float32))
    return 4.0 * sines * sines


def cas_table(positions, waves, length):
    product = positions[:, None] * waves[None, :] % length
    phase_angle = 2.0 * math.pi / length * product.astype(jnp.float32)
    return jnp.cos(phase_angle) + jnp.sin(phase_angle)


def wave_numbers(amount, length):
    indices = jnp.arange(amount, dtype=jnp.int32)
    live_mask = indices >= 0
    magnitude = jnp.minimum(indices, length - indices)
    return (indices, live_mask.astype(jnp.float32), magnitude)


def shards(state_field, to_modes, from_modes, mode_depth):
    wide_count = lax.axis_size("wide")
    wide_index = lax.axis_index("wide")
    lev_index = lax.axis_index("lev")
    levels, row_count, col_count = state_field.shape
    length = I + E
    ext_count = E // wide_count
    row_total = row_count + ext_count
    head_strip = spread(state_field[:, :2], "wide", 0)
    tail_strip = spread(state_field[:, row_count - 2 :], "wide", wide_count - 1)
    ext_slot = (wide_count - wide_index) % wide_count
    row_ids = ext_slot * ext_count + jnp.arange(ext_count, dtype=jnp.int32)
    fraction = (row_ids.astype(jnp.float32) + 1.0) / (E + 1.0)
    weights = tuple((weight[:, None] for weight in blend_weights(fraction)))
    end_val = tail_strip[:, 1:2]
    end_slope = tail_strip[:, 1:2] - tail_strip[:, 0:1]
    start_val = head_strip[:, 0:1]
    start_slope = head_strip[:, 1:2] - head_strip[:, 0:1]
    ext_block = hermite_mix(start_val, start_slope, end_val, end_slope, weights)
    stacked = jnp.concatenate([state_field, ext_block], axis=1)
    widened = extend_cols(stacked, E)
    waves, live_mask, magnitude = wave_numbers(length, length)
    lap_all = laplace(waves, length)
    positions = jnp.arange(length, dtype=jnp.int32)
    forward_x = cas_table(positions, waves, length) * live_mask[None, :]
    row_owner = positions // row_total
    local_row = positions % row_total
    ext_owner = (wide_count - row_owner) % wide_count
    row_pos = jnp.where(
        local_row < row_count,
        row_owner * row_count + local_row,
        I + ext_owner * ext_count + local_row - row_count,
    )
    forward_y = cas_table(row_pos, waves, length) * live_mask[None, :]
    inverse_y = forward_y.T / length
    inverse_x = forward_x[:I].T / length
    col_span = length // wide_count
    col_start = wide_index * col_span
    spec_x = jnp.einsum("irn,nc->irc", widened, forward_x, precision=highest)
    spectrum = jnp.einsum(
        "irc,rk->ick",
        lax.all_to_all(spec_x, "wide", split_axis=2, concat_axis=1, tiled=True),
        forward_y,
        precision=highest,
    )
    lev_start = lev_index * levels
    sub_block = lax.dynamic_slice(to_modes, (0, lev_start), (lax.axis_size("lev") * levels, levels))
    mode_values = lax.psum_scatter(
        jnp.einsum("ml,lck->mck", sub_block, spectrum, precision=highest),
        "lev",
        scatter_dimension=0,
        tiled=True,
    )
    lap_cols = lax.dynamic_slice_in_dim(lap_all, col_start, col_span)
    mag_cols = lax.dynamic_slice_in_dim(magnitude, col_start, col_span)
    live_cols = lax.dynamic_slice_in_dim(live_mask, col_start, col_span)
    inside = (
        mag_cols[:, None] * mag_cols[:, None] + magnitude[None, :] * magnitude[None, :] < KT * KT
    )
    keep_mask = live_cols[:, None] * live_mask[None, :] * inside.astype(jnp.float32)
    keep_mask, lap_sum = (keep_mask, lap_cols[:, None] + lap_all[None, :])
    mode_rates = lax.dynamic_slice_in_dim(mode_depth, lev_start, levels)
    solved = mode_values * keep_mask / (1.0 + mode_rates[:, None, None] * lap_sum)
    shard_piece = lax.all_gather(solved, "lev", axis=0, tiled=True)
    sub_block = lax.dynamic_slice(from_modes, (lev_start, 0), (levels, shard_piece.shape[0]))
    mixed_levels = jnp.einsum("lm,mck->lck", sub_block, shard_piece, precision=highest)
    rows_back = jnp.einsum("ick,kr->icr", mixed_levels, inverse_y, precision=highest)
    return jnp.einsum(
        "icr,cn->irn",
        lax.all_to_all(rows_back, "wide", split_axis=2, concat_axis=1, tiled=True)[
            :, :, :row_count
        ],
        inverse_x,
        precision=highest,
    )


def solution(mesh):
    placed = (P("lev", "wide", None), P(), P(), P())
    return jax.shard_map(
        shards, mesh=mesh, in_specs=placed, out_specs=P("lev", "wide", None), check_vma=False
    )
```

profile of v0, /device:TPU:1, one launch (start us, length us, event | category | flops | bytes accessed | tf_op | source)
XLA Modules:
  0.0 882.4 jit_solution(174005833860405015)
XLA Ops:
  6.5 0.0 copy-start
  6.5 0.0 all-reduce.3.cloned.1.call-start
  6.5 1.7 slice_select_fusion.1
  8.2 0.0 all-reduce.3.cloned.1.call-update
  8.3 501.3 %all-reduce.3.cloned.1.call-done = (f32[3,2,1472]{2,1,0:T(2,128)}, f32[3,2,1472]{2,1,0:T(2,128)}) async-done(((f32[3,2,1472]{2,1,0:T(2,128)}, f32[3,2,1472]{2,1,0:T(2,128)}), (f32[3,2,1472]{2,1,0:T(2,128)}, f32[3,2,1472]{2,1,0:T(2,128)})) %all-reduce.3.cloned.1.call-update) | async-done | bytes 70672 | tf_op jit(solution)/shard_map/psum | solution.py:18
  509.5 0.9 fusion.63
  510.5 1.1 fusion.61
  511.5 0.1 multiply_add_fusion
  511.6 1.1 fusion.116
  512.7 44.8 %fusion.10 = f32[3,24,1536]{2,1,0:T(8,128)} fusion(f32[3,24,1536]{2,1,0:T(8,128)S(1)} %fusion.116), kind=kOutput, calls=%fused_computation.13 | convolution fusion | flops 2062024704 | bytes 884736 | tf_op jit(solution)/shard_map/irn,nc->irc/dot_general | solution.py:108
  557.6 2.6 copy.20
  560.2 3.2 reshape.162
  563.5 6.0 all-to-all-start
  569.5 0.0 reduce-scatter.2.cloned.1.call-start
  569.6 12.6 %all-to-all-done = f32[64,1,1728]{2,1,0:T(1,128)S(1)} async-done(((f32[64,1,1728]{2,1,0:T(1,128)}), f32[64,1,1728]{2,1,0:T(1,128)S(1)}, u32[]{:S(2)}, u32[]{:S(2)}) %all-to-all-start) | async-done | bytes 442400 | tf_op jit(solution)/shard_map/all_to_all | solution.py:111
  582.2 0.5 broadcast.322
  582.7 2.5 reduce.8
  585.2 3.5 reshape.163
  588.7 2.8 copy.45
  591.5 2.8 all_to_all.29
  594.4 0.0 copy-start.1
  594.4 56.4 %fusion.8 = f32[3,24,1536]{2,1,0:T(8,128)S(1)} fusion(f32[3,1536,24]{1,2,0:T(8,128)S(1)} %all_to_all.29, s32[1536]{0:T(1024)S(1)} %fusion.76), kind=kOutput, calls=%fused_computation.11 | convolution fusion | flops 2062024704 | bytes 890880 | tf_op jit(solution)/shard_map/irc,rk->ick/dot_general | solution.py:109
  650.8 0.0 copy-done
  650.8 2.1 fusion.47
  652.9 2.2 copy.24
  655.2 0.0 reduce-scatter.2.cloned.1.call-update
  655.2 0.0 all-gather.2.cloned.1.call-start
  655.2 0.0 copy-done.1
  655.3 0.1 dynamic_slice.19
  655.3 0.1 multiply_multiply_fusion
  655.4 0.1 dynamic_slice.20
  655.5 0.1 dynamic-slice_multiply_fusion
  655.6 0.1 fusion.56
  655.7 63.5 %reduce-scatter.2.cloned.1.call-done = f32[3,24,1536]{2,1,0:T(8,128)} async-done(((f32[12,24,1536]{2,1,0:T(8,128)}), f32[3,24,1536]{2,1,0:T(8,128)}) %reduce-scatter.2.cloned.1.call-update) | async-done | bytes 442384 | tf_op jit(solution)/shard_map/reduce_scatter | solution.py:117
  719.1 1.9 add_divide_fusion
  721.0 0.0 all-gather.2.cloned.1.call-update
  721.1 27.4 %all-gather.2.cloned.1.call-done = f32[12,24,1536]{2,1,0:T(8,128)} async-done(((f32[3,24,1536]{2,1,0:T(8,128)}), f32[12,24,1536]{2,1,0:T(8,128)}) %all-gather.2.cloned.1.call-update) | async-done | bytes 1769488 | tf_op jit(solution)/shard_map/all_gather | solution.py:133
  748.4 3.7 fusion.45
  752.2 45.2 %fusion.6 = f32[3,24,1536]{2,1,0:T(8,128)} fusion(s32[1536]{0:T(1024)S(1)} %fusion.76, f32[3,24,1536]{2,0,1:T(4,128)S(1)} %fusion.45), kind=kOutput, calls=%fused_computation.9 | convolution fusion | flops 2064384000 | bytes 890880 | tf_op jit(solution)/shard_map/ick,kr->icr/dot_general | solution.py:136
  797.4 2.6 copy.27
  800.0 3.2 reshape.164
  803.3 10.4 %all-to-all-start.1 = ((f32[64,1,1728]{2,1,0:T(1,128)}), f32[64,1,1728]{2,1,0:T(1,128)S(1)}, u32[]{:S(2)}, u32[]{:S(2)}) async-start(f32[64,1,1728]{2,1,0:T(1,128)} %reshape.164), calls=%async_computation.2 | async-start | bytes 917504 | tf_op jit(solution)/shard_map/all_to_all | solution.py:139
  813.7 39.6 %sine_add_fusion = f32[1536,1536]{1,0:T(8,128)} fusion(), kind=kLoop, calls=%fused_computation.28 | loop fusion | flops 23592960 | bytes 9437184 | tf_op jit(solution)/shard_map/add | solution.py:60
  853.2 0.0 all-to-all-done.1
  853.2 2.5 reduce.9
  855.8 3.3 reshape.165
  859.1 2.8 copy.44
  861.8 2.8 all_to_all.33
  864.7 10.9 %fusion.33 = f32[3,23,1472]{2,1,0:T(8,128)} fusion(f32[1536,1536]{1,0:T(8,128)} %sine_add_fusion, f32[3,1536,24]{1,2,0:T(8,128)S(1)} %all_to_all.33), kind=kOutput, calls=%fused_computation.37 | convolution fusion | flops 1874362368 | bytes 9892608 | tf_op jit(solution)/shard_map/icr,cn->irn/dot_general | solution.py:137
  (5 shorter events, 0.1 us)
Async XLA Ops:
  6.5 644.3 %copy-start = (f32[12,12]{1,0:T(8,128)S(1)}, f32[12,12]{1,0:T(8,128)}, u32[]{:S(2)}) copy-start(f32[12,12]{1,0:T(8,128)} %param.5) | copy-start | bytes 1732
  6.5 503.0 %all-reduce.3.cloned.1.call-start = ((), (), s32[]{:S(2)}) async-start(), calls=%async_computation.5 | async-start | bytes 147456 | tf_op jit(solution)/shard_map/psum | solution.py:18
  563.5 18.7 %all-to-all-start = ((f32[64,1,1728]{2,1,0:T(1,128)}), f32[64,1,1728]{2,1,0:T(1,128)S(1)}, u32[]{:S(2)}, u32[]{:S(2)}) async-start(f32[64,1,1728]{2,1,0:T(1,128)} %reshape.162), calls=%async_computation | async-start | bytes 917504 | tf_op jit(solution)/shard_map/all_to_all | solution.py:111
  569.5 149.7 %reduce-scatter.2.cloned.1.call-start = ((), (), s32[]{:S(2)}) async-start(), calls=%async_computation.3 | async-start | bytes 2211840 | tf_op jit(solution)/shard_map/reduce_scatter | solution.py:117
  594.4 60.9 %copy-start.1 = (f32[12]{0:T(128)S(1)}, f32[12]{0:T(128)}, u32[]{:S(2)}) copy-start(f32[12]{0:T(128)} %param.7) | copy-start | bytes 148
  655.2 93.2 %all-gather.2.cloned.1.call-start = ((), (), s32[]{:S(2)}) async-start(), calls=%async_computation.4 | async-start | bytes 2211840 | tf_op jit(solution)/shard_map/all_gather | solution.py:133
  803.3 50.0 %all-to-all-start.1 = ((f32[64,1,1728]{2,1,0:T(1,128)}), f32[64,1,1728]{2,1,0:T(1,128)S(1)}, u32[]{:S(2)}, u32[]{:S(2)}) async-start(f32[64,1,1728]{2,1,0:T(1,128)} %reshape.164), calls=%async_computation.2 | async-start | bytes 917504 | tf_op jit(solution)/shard_map/all_to_all | solution.py:139
Sparse Core Ops, SparseCore 0:
  10.1 499.4 all-reduce.2
  655.3 63.7 reduce-scatter.1
  721.2 27.1 all-gather.1
where the time goes:
time: 892 us; the launch traced here: 882 us
  waiting for transfers between devices  605 us (68%)
  matrix products  163 us (18%)
  other arithmetic  51.7 us (6%)
  local copies, waits for them, and re-layouts  32.6 us (4%)
  starting transfers between devices  16.5 us (2%)
  between operations  13.7 us (2%)
    psum x1, waiting for transfers between devices, spread(): return lax.psum(block, axis)  501 us
    reduce_scatter x1, waiting for transfers between devices, shards(): lax.psum_scatter(jnp.einsum('ml,lck->mck', sub_block, spectrum, precision...  63.5 us
    dot_general x1, matrix products, shards(): jnp.einsum('irc,rk->ick', lax.all_to_all(spec_x, 'wide', split_axis=2, co...  56.4 us
    dot_general x1, matrix products, shards(): jnp.einsum('ick,kr->icr', mixed_levels, inverse_y, precision=highest)  45.2 us
    dot_general x1, matrix products, shards(): spec_x = jnp.einsum('irn,nc->irc', widened, forward_x, precision=highest)  44.8 us
    add x1, other arithmetic, cas_table(): return jnp.cos(phase_angle) + jnp.sin(phase_angle)  39.6 us
    all_gather x1, waiting for transfers between devices, shards(): shard_piece = lax.all_gather(solved, 'lev', axis=0, tiled=True)  27.4 us
  transfers between devices with their start and end apart: 5, of which 4 were waited for; matrix products, arithmetic and copies ran while one was open for 5% of the time, Pallas kernels for 0%

commit v1 on v0

v1 whole, which is shorter than its diff:
```python
import functools
import math

import jax
import jax.numpy as jnp
import ml_dtypes
import numpy as np
from jax import lax
from jax.experimental import pallas as pl
from jax.experimental.pallas import tpu as pltpu
from jax.sharding import PartitionSpec as P

I = 1472
E = 64
K = 12
KT = 512
N = I + E
W = 2 * KT
RING = 8
CROSS = 8
LEV = 4
LOC = 3
ROWS = 23
PAD = 24
PEERS = CROSS * LEV
COLS = 4
M = K * COLS
MESH = pl.DeviceIdType.MESH
F32 = jnp.float32
BF16 = jnp.bfloat16


def wave_of(position):
    return np.where(position < KT, position, position + N - W)


def pair(table):
    high = table.astype(ml_dtypes.bfloat16)
    low = (table - high.astype(np.float64)).astype(ml_dtypes.bfloat16)
    depth, width = table.shape
    blocks = width // 128
    both = np.stack([high.reshape(depth, blocks, 128), low.reshape(depth, blocks, 128)], axis=2)
    return np.ascontiguousarray(both.transpose(1, 0, 2, 3).reshape(blocks, depth, 256))


@functools.lru_cache(maxsize=None)
def tables():
    position = np.arange(W)
    waves = wave_of(position)
    angle = 2.0 * np.pi / N * ((np.arange(N)[:, None] * waves[None, :]) % N)
    cas = np.cos(angle) + np.sin(angle)
    f = (np.arange(E) + 1.0) / (E + 1.0)
    h00, h10 = 2 * f**3 - 3 * f**2 + 1, f**3 - 2 * f**2 + f
    h01, h11 = -2 * f**3 + 3 * f**2, f**3 - f**2
    forward = cas[:I].copy()
    forward[I - 1] += (h00 + h10) @ cas[I:]
    forward[I - 2] -= h10 @ cas[I:]
    forward[0] += (h01 - h11) @ cas[I:]
    forward[1] += h11 @ cas[I:]
    inverse = cas[:I].T / N

    fx = np.zeros((N, W))
    fx[:I] = forward
    lane = np.arange(256)
    ring, row = lane // PAD, lane % PAD
    good = (lane < RING * PAD) & (row < ROWS)
    source = ROWS * (np.arange(CROSS)[:, None] * RING + ring[None, :]) + row[None, :]
    source = np.where(good[None, :], source, 0).reshape(-1)
    good = np.tile(good, CROSS)
    fy = np.where(good[:, None], forward[source], 0.0)
    iy = np.where(good[None, :], inverse[:, source], 0.0)
    ix = np.zeros((W, N))
    ix[:, :I] = inverse
    magnitude = np.minimum(waves, N - waves)
    lap = 4.0 * np.sin(np.pi * waves / N) ** 2
    line = np.zeros((8, W), np.float32)
    line[0], line[1] = lap, magnitude
    return pair(fx), pair(fy), pair(iy), pair(ix), line


def split(value):
    high = value.astype(BF16)
    return high, (value - high.astype(F32)).astype(BF16)


def total(product, rows):
    return (
        (product[rows:, 128:] + product[:rows, 128:]) + product[rows:, :128]
    ) + product[:rows, :128]


def kernel(
    x_ref, to_ref, from_ref, depth_ref, line_ref, fx_hbm, fy_hbm, iy_hbm, ix_hbm, out_ref,
    fx, fy, iy, ix, xf, xs, ys, ms, zs,
    send_a, recv_a, send_b, recv_b, send_c, recv_c, send_d, recv_d,
    fx_sem, table_sem, sa_sem, ra_sem, sb_sem, rb_sem, sc_sem, rc_sem, sd_sem, rd_sem,
):
    wide = lax.axis_index("wide")
    lev = lax.axis_index("lev")
    ring = lax.rem(wide, RING)
    cross = lax.div(wide, RING)
    me = cross * LEV + lev

    def ring_id(z):
        return {"wide": cross * RING + z, "lev": lev}

    def peer_id(s):
        return {"wide": lax.div(s, LEV) * RING + ring, "lev": lax.rem(s, LEV)}

    order = [lax.rem(ring + step, RING) for step in (4, 3, 5, 2, 6, 1, 7, 0)]

    fx_copies = []
    for n, z in enumerate(order):
        copy = pltpu.make_async_copy(fx_hbm.at[z], fx.at[n], fx_sem.at[n])
        copy.start()
        fx_copies.append(copy)
    rest = [
        pltpu.make_async_copy(source, target, table_sem.at[n])
        for n, (source, target) in enumerate(((fy_hbm, fy), (iy_hbm, iy), (ix_hbm, ix)))
    ]

    barrier = pltpu.get_barrier_semaphore()
    for z in order[:-1]:
        pl.semaphore_signal(barrier, inc=1, device_id=ring_id(z), device_id_type=MESH)

    @pl.loop(1, PEERS)
    def _(step):
        s = lax.rem(me + step, PEERS)
        pl.semaphore_signal(barrier, inc=1, device_id=peer_id(s), device_id_type=MESH)

    for copy in rest:
        copy.start()

    xf[...] = jnp.zeros_like(xf)
    for l in range(LOC):
        xf[l * PAD : l * PAD + ROWS, :I] = x_ref[l]
    high, low = split(xf[...])
    xs[:80] = high
    xs[80:] = low

    pl.semaphore_wait(barrier, RING - 1 + PEERS - 1)

    def ring_copy(z, l):
        rows = pl.ds(l * PAD, PAD)
        return pltpu.make_async_remote_copy(
            src_ref=send_a.at[z, rows],
            dst_ref=recv_a.at[l, ring],
            send_sem=sa_sem,
            recv_sem=ra_sem.at[l],
            device_id=ring_id(z),
            device_id_type=MESH,
        )

    for n, z in enumerate(order):
        fx_copies[n].wait()
        block = total(jnp.dot(xs[...], fx[n], preferred_element_type=F32), 80)[: LOC * PAD]
        if n < RING - 1:
            send_a[z] = block
            ring_copy(z, 0).start()
        else:
            for l in range(LOC):
                recv_a[l, ring] = block[l * PAD : (l + 1) * PAD]
    for l in range(1, LOC):
        for z in order[:-1]:
            ring_copy(z, l).start()

    row = lax.broadcasted_iota(jnp.int32, (M, 1), 0)
    level_of_row = lax.div(lax.rem(row, 16), COLS) * LOC + lax.div(row, 16)
    pick = (level_of_row == lax.broadcasted_iota(jnp.int32, (M, K), 1)).astype(F32)
    same = (
        lax.rem(row, COLS) == lax.rem(lax.broadcasted_iota(jnp.int32, (M, M), 1), COLS)
    ).astype(F32)

    def expand(small):
        tall = jnp.dot(pick, small, preferred_element_type=F32, precision=lax.Precision.HIGHEST)
        full = lax.dot_general(
            tall, pick, (((1,), (1,)), ((), ())),
            preferred_element_type=F32, precision=lax.Precision.HIGHEST,
        )
        return full * same

    to_big = expand(to_ref[...])
    from_big = expand(from_ref[...])
    depth = jnp.sum(pick * depth_ref[...], axis=1, keepdims=True)
    column = ring * 128 + me * COLS + lax.rem(row, COLS)
    hit = lax.broadcasted_iota(jnp.int32, (M, W), 1) == column
    lap_q = jnp.sum(jnp.where(hit, line_ref[0:1], 0.0), axis=1, keepdims=True)
    mag_q = jnp.sum(jnp.where(hit, line_ref[1:2], 0.0), axis=1, keepdims=True)
    top = lax.broadcasted_iota(jnp.int32, (8, 128), 0) < COLS

    def cross_copy(l, s):
        return pltpu.make_async_remote_copy(
            src_ref=send_b.at[l, s],
            dst_ref=recv_b.at[l, me],
            send_sem=sb_sem,
            recv_sem=rb_sem.at[l],
            device_id=peer_id(s),
            device_id_type=MESH,
        )

    def bulk(ref, sem):
        return pltpu.make_async_copy(ref, ref, sem)

    for l in range(LOC):
        bulk(recv_a.at[l, pl.ds(0, RING - 1)], ra_sem.at[l]).wait()
        rows = recv_a[l].reshape(RING * PAD, 128)
        first = rows[:128].T
        second = jnp.concatenate([rows[128:], jnp.zeros((64, 128), F32)], axis=0).T
        for g in range(PEERS // 2):
            a, b = first[8 * g : 8 * g + 8], second[8 * g : 8 * g + 8]
            send_b[l, 2 * g] = jnp.where(top, a, pltpu.roll(b, 4, 0))
            send_b[l, 2 * g + 1] = jnp.where(top, pltpu.roll(a, 4, 0), b)
        recv_b[l, me] = send_b[l, me]

        @pl.loop(1, PEERS)
        def _(step):
            cross_copy(l, lax.rem(me + step, PEERS)).start()

    for l in range(LOC):
        bulk(recv_b.at[l, pl.ds(0, PEERS - 1)], rb_sem.at[l]).wait()
        for c in range(CROSS):
            v = [recv_b[l, c * LEV + k] for k in range(LEV)]
            a = [jnp.where(top, v[k], pltpu.roll(v[k + 1], 4, 0)) for k in (0, 2)]
            b = [jnp.where(top, pltpu.roll(v[k], 4, 0), v[k + 1]) for k in (0, 2)]
            for t, half in enumerate((a, b)):
                high, low = split(jnp.concatenate(half, axis=0))
                lanes = slice((2 * c + t) * 128, (2 * c + t + 1) * 128)
                ys[16 * l : 16 * l + 16, lanes] = high
                ys[M + 16 * l : M + 16 * l + 16, lanes] = low

    rest[0].wait()

    @pl.loop(0, RING)
    def _(j):
        lanes = pl.ds(pl.multiple_of(j * 128, 128), 128)
        spectrum = total(jnp.dot(ys[...], fy[j], preferred_element_type=F32), M)
        modes = jnp.dot(to_big, spectrum, preferred_element_type=F32, precision=lax.Precision.HIGHEST)
        lap_p = line_ref[0:1, lanes]
        mag_p = line_ref[1:2, lanes]
        keep = (mag_p * mag_p + mag_q * mag_q < float(KT * KT)).astype(F32)
        solved = modes * keep / (1.0 + depth * (lap_p + lap_q))
        mixed = jnp.dot(from_big, solved, preferred_element_type=F32, precision=lax.Precision.HIGHEST)
        high, low = split(mixed)
        ms[:M, lanes] = high
        ms[M:, lanes] = low

    rest[1].wait()

    def back_copy(l, s):
        return pltpu.make_async_remote_copy(
            src_ref=send_c.at[l, s],
            dst_ref=recv_c.at[l, me],
            send_sem=sc_sem,
            recv_sem=rc_sem.at[l],
            device_id=peer_id(s),
            device_id_type=MESH,
        )

    @pl.loop(0, CROSS)
    def _(step):
        c = lax.rem(cross + 1 + step, CROSS)
        half = [
            total(jnp.dot(ms[...], iy[2 * c + t], preferred_element_type=F32), M)
            for t in range(2)
        ]
        for l in range(LOC):
            for k in (0, 2):
                at = 16 * l + 4 * k
                a, b = half[0][at : at + 8], half[1][at : at + 8]
                send_c[l, c * LEV + k] = jnp.where(top, a, pltpu.roll(b, 4, 0))
                send_c[l, c * LEV + k + 1] = jnp.where(top, pltpu.roll(a, 4, 0), b)

        @pl.when(step < CROSS - 1)
        def _():
            for k in range(LEV):
                back_copy(0, c * LEV + k).start()

    for k in range(1, LEV):
        back_copy(0, cross * LEV + lax.rem(lev + k, LEV)).start()
    for l in range(LOC):
        recv_c[l, me] = send_c[l, me]
        if l:

            @pl.loop(1, PEERS)
            def _(step):
                back_copy(l, lax.rem(me + step, PEERS)).start()

    def home_copy(l, z):
        return pltpu.make_async_remote_copy(
            src_ref=send_d.at[l, z],
            dst_ref=recv_d.at[ring, l],
            send_sem=sd_sem,
            recv_sem=rd_sem,
            device_id=ring_id(z),
            device_id_type=MESH,
        )

    for l in range(LOC):
        bulk(recv_c.at[l, pl.ds(0, PEERS - 1)], rc_sem.at[l]).wait()
        first, second = [], []
        for g in range(PEERS // 2):
            a, b = recv_c[l, 2 * g], recv_c[l, 2 * g + 1]
            first.append(jnp.where(top, a, pltpu.roll(b, 4, 0)))
            second.append(jnp.where(top, pltpu.roll(a, 4, 0), b))
        rows = jnp.concatenate(
            [jnp.concatenate(first, axis=0).T, jnp.concatenate(second, axis=0).T[:64]], axis=0
        )
        send_d[l] = rows.reshape(RING, PAD, 128)
        recv_d[ring, l] = send_d[l, ring]
        for z in order[:-1]:
            home_copy(l, z).start()

    bulk(recv_d.at[pl.ds(0, RING - 1)], rd_sem).wait()
    for z in range(RING):
        block = recv_d[z].reshape(LOC * PAD, 128)
        high, low = split(jnp.concatenate([block, jnp.zeros((8, 128), F32)], axis=0))
        zs[:80, z * 128 : (z + 1) * 128] = high
        zs[80:, z * 128 : (z + 1) * 128] = low

    rest[2].wait()
    for j in range(N // 128):
        field = total(jnp.dot(zs[...], ix[j], preferred_element_type=F32), 80)
        width = min(128, I - j * 128)
        for l in range(LOC):
            out_ref[l, :, j * 128 : j * 128 + width] = field[l * PAD : l * PAD + ROWS, :width]

    bulk(send_a.at[pl.ds(0, RING - 1)], sa_sem).wait()
    for l in range(LOC):
        bulk(send_b.at[l, pl.ds(0, PEERS - 1)], sb_sem).wait()
        bulk(send_c.at[l, pl.ds(0, PEERS - 1)], sc_sem).wait()
        bulk(send_d.at[l, pl.ds(0, RING - 1)], sd_sem).wait()


def shards(state_field, to_modes, from_modes, mode_depth):
    fx, fy, iy, ix, line = (jnp.asarray(table) for table in tables())
    vmem = pl.BlockSpec(memory_space=pltpu.VMEM)
    hbm = pl.BlockSpec(memory_space=pl.ANY)
    dma = pltpu.SemaphoreType.DMA
    return pl.pallas_call(
        kernel,
        out_shape=jax.ShapeDtypeStruct((LOC, ROWS, I), F32),
        in_specs=[vmem] * 5 + [hbm] * 4,
        out_specs=vmem,
        scratch_shapes=[
            pltpu.VMEM(fx.shape, BF16),
            pltpu.VMEM(fy.shape, BF16),
            pltpu.VMEM(iy.shape, BF16),
            pltpu.VMEM(ix.shape, BF16),
            pltpu.VMEM((80, N), F32),
            pltpu.VMEM((160, N), BF16),
            pltpu.VMEM((2 * M, CROSS * 256), BF16),
            pltpu.VMEM((2 * M, W), BF16),
            pltpu.VMEM((160, W), BF16),
            pltpu.VMEM((RING, LOC * PAD, 128), F32),
            pltpu.VMEM((LOC, RING, PAD, 128), F32),
            pltpu.VMEM((LOC, PEERS, 8, 128), F32),
            pltpu.VMEM((LOC, PEERS, 8, 128), F32),
            pltpu.VMEM((LOC, PEERS, 8, 128), F32),
            pltpu.VMEM((LOC, PEERS, 8, 128), F32),
            pltpu.VMEM((LOC, RING, PAD, 128), F32),
            pltpu.VMEM((RING, LOC, PAD, 128), F32),
            dma((RING,)),
            dma((3,)),
            dma,
            dma((LOC,)),
            dma,
            dma((LOC,)),
            dma,
            dma((LOC,)),
            dma,
            dma,
        ],
        compiler_params=pltpu.CompilerParams(
            collective_id=0, has_side_effects=True, vmem_limit_bytes=56 * 2**20
        ),
        cost_estimate=pl.CostEstimate(flops=4 * 10**9, bytes_accessed=32 * 10**6, transcendentals=0),
    )(state_field, to_modes, from_modes, mode_depth.reshape(1, K), line, fx, fy, iy, ix)


def solution(mesh):
    assert dict(mesh.shape) == {"wide": RING * CROSS, "lev": LEV}
    placed = (P("lev", "wide", None), P(), P(), P())
    return jax.shard_map(
        shards, mesh=mesh, in_specs=placed, out_specs=P("lev", "wide", None), check_vma=False
    )
```

time: 892 us -> 51.9 us (0.06); the launches traced: 882 us -> 51.8 us
  waiting for transfers between devices: 605 us -> 0 us
  matrix products: 163 us -> 0 us
  other arithmetic: 51.7 us -> 0 us
  Pallas kernels: 0 us -> 50 us
  local copies, waits for them, and re-layouts: 32.6 us -> 1.8 us
  starting transfers between devices: 16.5 us -> 0 us
  between operations: 13.7 us -> 0.01 us
    psum x1 -> x0, waiting for transfers between devices: 501 us -> none  [spread(): return lax.psum(block, axis)]
    dot_general x6 -> x0, matrix products: 163 us -> none  [the longest x1 56.4 us: shards(): jnp.einsum('irc,rk->ick', lax.all_to_all(spec_x, 'wide', split_axis=2, co...]
    reduce_scatter x1 -> x0, waiting for transfers between devices: 63.5 us -> none  [shards(): lax.psum_scatter(jnp.einsum('ml,lck->mck', sub_block, spectrum, precision...]
    pallas_call x0 -> x1, Pallas kernels: none -> 50 us  [shards(): pl.pallas_call(kernel, out_shape=jax.ShapeDtypeStruct((LOC, ROWS, I), F32...]
    add x5 -> x0, other arithmetic: 40.6 us -> none  [the longest x1 39.6 us: cas_table(): return jnp.cos(phase_angle) + jnp.sin(phase_angle)]
    all_gather x1 -> x0, waiting for transfers between devices: 27.4 us -> none  [shards(): shard_piece = lax.all_gather(solved, 'lev', axis=0, tiled=True)]
    all_to_all x2 -> x0, starting transfers between devices: 16.4 us -> none  [the longest x1 10.4 us: shards(): lax.all_to_all(rows_back, 'wide', split_axis=2, concat_axis=1, tiled=True)]
    all_to_all x2 -> x0, waiting for transfers between devices: 12.6 us -> none  [the longest x1 12.6 us: shards(): lax.all_to_all(spec_x, 'wide', split_axis=2, concat_axis=1, tiled=True)]
  transfers between devices with their start and end apart: 5 -> 0, of which waited for: 4 -> 0; matrix products, arithmetic and copies ran while one was open for 5% -> 0% of each run, Pallas kernels for 0% -> 0%
where the time goes in v1:
time: 51.9 us; the launch traced here: 51.8 us
  Pallas kernels  50 us (96%)
  local copies, waits for them, and re-layouts  1.8 us (3%)
    pallas_call x1, Pallas kernels, shards(): pl.pallas_call(kernel, out_shape=jax.ShapeDtypeStruct((LOC, ROWS, I), F32...  50 us
    unnamed x1, local copies, waits for them, and re-layouts  1.8 us

profile of v1, /device:TPU:1, one launch (start us, length us, event | category | flops | bytes accessed | tf_op | source)
XLA Modules:
  0.0 51.8 jit_solution(10786612715423718093)
XLA Ops:
  0.0 50.0 %shard_map.91 = f32[3,23,1472]{2,1,0:T(8,128)} custom-call(f32[3,23,1472]{2,1,0:T(8,128)} %x_ref.1, f32[12,12]{1,0:T(8,128)} %to_ref.1, f32[12,12]{1,0:T(8,128)} %from_ref.1, f32[1,12]{1,0:T(1,128)} %bitcast.1, f32[8,1024]{1,0:T(8,128)} %constant.14.clone.line_ref, bf16[8,1536,256]{2,1,0:T(8,128)(2,1)} %constant.10.clone.fx_hbm, ...), custom_call_target="tpu_custom_call" | custom-call | flops 4000000000 | bytes 32000000 | tf_op jit(solution)/shard_map/pallas_call | solution.py:339
  50.0 1.8 %copy.11 = f32[3,23,1472]{2,1,0:T(8,128)} copy(f32[3,23,1472]{2,1,0:T(8,128)} %shard_map.91) | data formatting | bytes 812544

commit v2 on v1

v2 whole, which is shorter than its diff:
```python
import functools
import math

import jax
import jax.numpy as jnp
import ml_dtypes
import numpy as np
from jax import lax
from jax.experimental import pallas as pl
from jax.experimental.pallas import tpu as pltpu
from jax.sharding import PartitionSpec as P

I = 1472
E = 64
K = 12
KT = 512
N = I + E
W = 2 * KT
RING = 8
WIDE = 64
LEV = 4
CHIPS = 128
LOC = 3
ROWS = 23
PAD = 24
COLS = 4
LAST = 5
M = K * COLS
MESH = pl.DeviceIdType.MESH
F32 = jnp.float32
BF16 = jnp.bfloat16


def wave_of(position):
    return np.where(position < KT, position, position + N - W)


def pair(table):
    high = table.astype(ml_dtypes.bfloat16)
    low = (table - high.astype(np.float64)).astype(ml_dtypes.bfloat16)
    depth, width = table.shape
    blocks = width // 128
    both = np.stack([high.reshape(depth, blocks, 128), low.reshape(depth, blocks, 128)], axis=2)
    return np.ascontiguousarray(both.transpose(1, 0, 2, 3).reshape(blocks, depth, 256))


@functools.lru_cache(maxsize=None)
def tables():
    position = np.arange(W)
    waves = wave_of(position)
    angle = 2.0 * np.pi / N * ((np.arange(N)[:, None] * waves[None, :]) % N)
    cas = np.cos(angle) + np.sin(angle)
    f = (np.arange(E) + 1.0) / (E + 1.0)
    h00, h10 = 2 * f**3 - 3 * f**2 + 1, f**3 - 2 * f**2 + f
    h01, h11 = -2 * f**3 + 3 * f**2, f**3 - f**2
    forward = cas[:I].copy()
    forward[I - 1] += (h00 + h10) @ cas[I:]
    forward[I - 2] -= h10 @ cas[I:]
    forward[0] += (h01 - h11) @ cas[I:]
    forward[1] += h11 @ cas[I:]
    inverse = cas[:I].T / N

    fx = np.zeros((N, W))
    fx[:I] = forward
    index, device = np.arange(N) // WIDE, np.arange(N) % WIDE
    good = index < ROWS
    source = np.where(good, ROWS * device + index, 0)
    fy = np.where(good[:, None], forward[source], 0.0)
    iy = np.where(good[None, :], inverse[:, source], 0.0)
    ix = np.zeros((W, N))
    ix[:, :I] = inverse
    ix = np.stack([pair(ix[: W // 2]), pair(ix[W // 2 :])])
    magnitude = np.minimum(waves, N - waves)
    lap = 4.0 * np.sin(np.pi * waves / N) ** 2
    line = np.zeros((8, W), np.float32)
    line[0], line[1] = lap, magnitude
    return pair(fx), pair(fy), pair(iy), ix, line


def split(value):
    high = value.astype(BF16)
    return high, (value - high.astype(F32)).astype(BF16)


def total(product, rows):
    return (
        (product[rows:, 128:] + product[:rows, 128:]) + product[rows:, :128]
    ) + product[:rows, :128]


def split_three(value):
    high, rest = value.astype(BF16), value
    rest = rest - high.astype(F32)
    middle = rest.astype(BF16)
    return high, middle, (rest - middle.astype(F32)).astype(BF16)


def kernel(
    x_ref, to_ref, from_ref, depth_ref, line_ref, fx_hbm, fy_hbm, iy_hbm, ix_hbm, out_ref,
    fx, fy, iy, ix, xf, xs, ys, qs, ms, zs, part,
    swap_x, spec_x, send_a, recv_a, mid_a, mid_b, send_b, recv_b, home, other,
    fx_sem, table_sem, swap_sem, s1_sem, s2_sem, r2_sem, s3_sem, r3_sem, all_sem,
):
    wide = lax.axis_index("wide")
    lev = lax.axis_index("lev")
    core = lev & 1
    half = lev >> 1
    ring = wide & (RING - 1)
    me = half * WIDE + wide
    partner = {"wide": wide, "lev": lev ^ 1}

    def chip(s):
        return {"wide": s & (WIDE - 1), "lev": ((s >> 6) << 1) + core}

    def across(q):
        return chip((q << 3) + ring)

    cross = me >> 3

    blocks = [(core ^ 1) * COLS + c for c in range(COLS)] + [core * COLS + c for c in range(COLS)]
    fx_copies = []
    for n, block in enumerate(blocks):
        copy = pltpu.make_async_copy(fx_hbm.at[block], fx.at[n], fx_sem.at[n])
        copy.start()
        fx_copies.append(copy)
    rest = [
        pltpu.make_async_copy(source, target, table_sem.at[n])
        for n, (source, target) in enumerate(((fy_hbm, fy), (iy_hbm, iy), (ix_hbm, ix)))
    ]

    barrier = pltpu.get_barrier_semaphore()
    for step in range(1, RING):
        z = (ring + step) & (RING - 1)
        pl.semaphore_signal(
            barrier, inc=1, device_id=chip(me - ring + z), device_id_type=MESH
        )
    for step in range(1, 16):
        pl.semaphore_signal(
            barrier, inc=1, device_id=across((cross + step) & 15), device_id_type=MESH
        )
    pl.semaphore_signal(barrier, inc=1, device_id=partner, device_id_type=MESH)

    for copy in rest:
        copy.start()

    xf[...] = jnp.zeros_like(xf)
    for l in range(LOC):
        xf[l * PAD : l * PAD + ROWS, :I] = x_ref[l]
    high, low = split(xf[...])
    xs[:80] = high
    xs[80:] = low

    def swap_copy(c):
        return pltpu.make_async_remote_copy(
            src_ref=swap_x.at[c],
            dst_ref=spec_x.at[pl.ds(core * LOC, LOC), c],
            send_sem=s1_sem,
            recv_sem=swap_sem,
            device_id=partner,
            device_id_type=MESH,
        )

    for n in range(2 * COLS):
        fx_copies[n].wait()
        block = total(jnp.dot(xs[...], fx[n], preferred_element_type=F32), 80)[: LOC * PAD]
        block = block.reshape(LOC, PAD, 128)
        if n < COLS:
            swap_x[n] = block
            if n == 0:
                pl.semaphore_wait(barrier, RING - 1 + 15 + 1)
                for step in range(1, 16):
                    pl.semaphore_signal(
                        all_sem, inc=1, device_id=across((cross + step) & 15), device_id_type=MESH
                    )
            swap_copy(n).start()
        else:
            for l in range(LOC):
                spec_x[core * LOC + l, n - COLS] = block[l]

    def bulk(ref, sem):
        return pltpu.make_async_copy(ref, ref, sem)

    bulk(spec_x.at[pl.ds(0, LOC)], swap_sem).wait()

    def pack(rows, buffer):
        last = rows(LAST)
        for l in range(LAST):
            tail = last[32 * l : 32 * l + 32] if l < 3 else jnp.zeros((32, 128), F32)
            buffer[pl.ds(l, CHIPS, stride=8), :] = jnp.concatenate([rows(l), tail], axis=0).T

    def unpack(buffer, store):
        for l in range(LAST):
            rows = buffer[pl.ds(l, CHIPS, stride=8), :].T
            store(l, 0, rows[:96])
            if l < 3:
                store(LAST, 32 * l, rows[96:])

    pack(lambda l: spec_x[l].reshape(96, 128), send_a)

    def exchange(source, target, send_sem, recv_sem):
        def copy(s):
            return pltpu.make_async_remote_copy(
                src_ref=source.at[pl.ds(pl.multiple_of(s * 8, 8), LAST)],
                dst_ref=target.at[pl.ds(pl.multiple_of(me * 8, 8), LAST)],
                send_sem=send_sem,
                recv_sem=recv_sem,
                device_id=chip(s),
                device_id_type=MESH,
            )

        @pl.loop(1, CHIPS)
        def _(step):
            copy((me + step) & (CHIPS - 1)).start()

        own = pl.ds(pl.multiple_of(me * 8, 8), 8)
        target[own, :] = source[own, :]

    def arrived(buffer, sem):
        bulk(buffer.at[pl.ds(0, (CHIPS - 1) * LAST)], sem).wait()

    pl.semaphore_wait(all_sem, 15)
    exchange(send_a, recv_a, s2_sem, r2_sem)

    row = lax.broadcasted_iota(jnp.int32, (M, 1), 0)
    pick = ((row >> 2) == lax.broadcasted_iota(jnp.int32, (M, K), 1)).astype(F32)
    turn = lax.broadcasted_iota(jnp.int32, (6 * M, 1), 0)
    turn = lax.rem(turn, M) >> 2
    pick_six = (turn == lax.broadcasted_iota(jnp.int32, (6 * M, K), 1)).astype(F32)
    lane = lax.broadcasted_iota(jnp.int32, (M, 6 * M), 1)
    same = (row & 3) == (lane & 3)

    def expand(small):
        tall = jnp.dot(pick, small, preferred_element_type=F32, precision=lax.Precision.HIGHEST)
        full = lax.dot_general(
            tall, pick_six, (((1,), (1,)), ((), ())),
            preferred_element_type=F32, precision=lax.Precision.HIGHEST,
        )
        full = jnp.where(same, full, 0.0)
        high = full.astype(BF16).astype(F32)
        middle = (full - high).astype(BF16).astype(F32)
        low = full - high - middle
        return jnp.where(lane < 3 * M, high, jnp.where(lane < 5 * M, middle, low)).astype(BF16)

    to_big = expand(to_ref[...])
    from_big = expand(from_ref[...])
    depth = jnp.sum(pick * depth_ref[...], axis=1, keepdims=True)
    column = core * (W // 2) + (row & 3) * CHIPS + me
    hit = lax.broadcasted_iota(jnp.int32, (M, W), 1) == column
    lap_q = jnp.sum(jnp.where(hit, line_ref[0:1], 0.0), axis=1, keepdims=True)
    mag_q = jnp.sum(jnp.where(hit, line_ref[1:2], 0.0), axis=1, keepdims=True)
    left = lax.broadcasted_iota(jnp.int32, (M // 2, 128), 1) < WIDE

    def mix(matrix, value):
        high, middle, low = split_three(value)
        for n, piece in enumerate((high, middle, low, high, middle, high)):
            qs[n * M : (n + 1) * M] = piece
        return jnp.dot(matrix, qs[...], preferred_element_type=F32)

    arrived(recv_a, r2_sem)

    def store_a(l, at, rows):
        mid_a[l * 96 + at : l * 96 + at + rows.shape[0]] = rows

    unpack(recv_a, store_a)
    for t in range(PAD // 2):
        a = mid_a[pl.ds(2 * t, M // 2, stride=PAD), :]
        b = mid_a[pl.ds(2 * t + 1, M // 2, stride=PAD), :]
        first = jnp.where(left, a, pltpu.roll(b, WIDE, 1))
        second = jnp.where(left, pltpu.roll(a, WIDE, 1), b)
        high, low = split(jnp.concatenate([first, second], axis=0))
        ys[:M, t * 128 : t * 128 + 128] = high
        ys[M:, t * 128 : t * 128 + 128] = low

    rest[0].wait()

    @pl.loop(0, W // 256)
    def _(j):
        lanes = pl.ds(pl.multiple_of(j * 256, 256), 256)
        spectrum = jnp.concatenate(
            [
                total(jnp.dot(ys[...], fy[2 * j + n], preferred_element_type=F32), M)
                for n in range(2)
            ],
            axis=1,
        )
        modes = mix(to_big, spectrum)
        lap_p = line_ref[0:1, lanes]
        mag_p = line_ref[1:2, lanes]
        keep = (mag_p * mag_p + mag_q * mag_q < float(KT * KT)).astype(F32)
        solved = modes * keep / (1.0 + depth * (lap_p + lap_q))
        high, low = split(mix(from_big, solved))
        ms[:M, lanes] = high
        ms[M:, lanes] = low

    rest[1].wait()
    for t in range(PAD // 2):
        value = total(jnp.dot(ms[...], iy[t], preferred_element_type=F32), M)
        first, second = value[: M // 2], value[M // 2 :]
        mid_b[pl.ds(2 * t, M // 2, stride=PAD), :] = jnp.where(
            left, first, pltpu.roll(second, WIDE, 1)
        )
        mid_b[pl.ds(2 * t + 1, M // 2, stride=PAD), :] = jnp.where(
            left, pltpu.roll(first, WIDE, 1), second
        )
    pack(lambda l: mid_b[l * 96 : l * 96 + 96], send_b)
    exchange(send_b, recv_b, s3_sem, r3_sem)
    rest[2].wait()
    arrived(recv_b, r3_sem)

    def store_b(l, at, rows):
        home[l, at : at + rows.shape[0]] = rows

    unpack(recv_b, store_b)
    back = pltpu.make_async_remote_copy(
        src_ref=home.at[pl.ds((core ^ 1) * LOC, LOC)],
        dst_ref=other,
        send_sem=table_sem.at[3],
        recv_sem=table_sem.at[4],
        device_id=partner,
        device_id_type=MESH,
    )
    back.start()

    def gather(level):
        for c in range(COLS):
            rows = [level(l)[PAD * c : PAD * c + PAD] for l in range(LOC)]
            high, low = split(jnp.concatenate(rows + [jnp.zeros((8, 128), F32)], axis=0))
            zs[:80, c * 128 : c * 128 + 128] = high
            zs[80:, c * 128 : c * 128 + 128] = low

    gather(lambda l: home[core * LOC + l])
    for j in range(N // 128):
        part[:, j * 128 : j * 128 + 128] = total(
            jnp.dot(zs[...], ix[core, j], preferred_element_type=F32), 80
        )
    back.wait_recv()
    gather(lambda l: other[l])
    for j in range(N // 128):
        field = total(jnp.dot(zs[...], ix[core ^ 1, j], preferred_element_type=F32), 80)
        field = field + part[:, j * 128 : j * 128 + 128]
        width = min(128, I - j * 128)
        for l in range(LOC):
            out_ref[l, :, j * 128 : j * 128 + width] = field[l * PAD : l * PAD + ROWS, :width]

    bulk(swap_x, s1_sem).wait()
    arrived(send_a, s2_sem)
    arrived(send_b, s3_sem)
    back.wait_send()


def shards(state_field, to_modes, from_modes, mode_depth):
    fx, fy, iy, ix, line = (jnp.asarray(table) for table in tables())
    vmem = pl.BlockSpec(memory_space=pltpu.VMEM)
    hbm = pl.BlockSpec(memory_space=pl.ANY)
    dma = pltpu.SemaphoreType.DMA
    return pl.pallas_call(
        kernel,
        out_shape=jax.ShapeDtypeStruct((LOC, ROWS, I), F32),
        in_specs=[vmem] * 5 + [hbm] * 4,
        out_specs=vmem,
        scratch_shapes=[
            pltpu.VMEM(fx.shape, BF16),
            pltpu.VMEM(fy.shape, BF16),
            pltpu.VMEM(iy.shape, BF16),
            pltpu.VMEM(ix.shape, BF16),
            pltpu.VMEM((80, N), F32),
            pltpu.VMEM((160, N), BF16),
            pltpu.VMEM((2 * M, N), BF16),
            pltpu.VMEM((6 * M, 256), BF16),
            pltpu.VMEM((2 * M, W), BF16),
            pltpu.VMEM((160, W // 2), BF16),
            pltpu.VMEM((80, N), F32),
            pltpu.VMEM((COLS, LOC, PAD, 128), F32),
            pltpu.VMEM((2 * LOC, COLS, PAD, 128), F32),
            pltpu.VMEM((8 * CHIPS, 128), F32),
            pltpu.VMEM((8 * CHIPS, 128), F32),
            pltpu.VMEM((2 * LOC * 96, 128), F32),
            pltpu.VMEM((2 * LOC * 96, 128), F32),
            pltpu.VMEM((8 * CHIPS, 128), F32),
            pltpu.VMEM((8 * CHIPS, 128), F32),
            pltpu.VMEM((2 * LOC, 96, 128), F32),
            pltpu.VMEM((LOC, 96, 128), F32),
            dma((2 * COLS,)),
            dma((5,)),
            dma,
            dma,
            dma,
            dma,
            dma,
            dma,
            pltpu.SemaphoreType.REGULAR,
        ],
        compiler_params=pltpu.CompilerParams(
            collective_id=0, has_side_effects=True, vmem_limit_bytes=56 * 2**20
        ),
        cost_estimate=pl.CostEstimate(flops=4 * 10**9, bytes_accessed=27 * 10**6, transcendentals=0),
    )(state_field, to_modes, from_modes, mode_depth.reshape(1, K), line, fx, fy, iy, ix)


def solution(mesh):
    assert dict(mesh.shape) == {"wide": WIDE, "lev": LEV}
    placed = (P("lev", "wide", None), P(), P(), P())
    return jax.shard_map(
        shards, mesh=mesh, in_specs=placed, out_specs=P("lev", "wide", None), check_vma=False
    )
```

time: 51.9 us -> 45 us (0.87)
  Pallas kernels: 50 us -> 43 us
    pallas_call x1, Pallas kernels: 50 us -> 43 us  [shards(): pl.pallas_call(kernel, out_shape=jax.ShapeDtypeStruct((LOC, ROWS, I), F32...]
where the time goes in v2:
time: 45 us; the launch traced here: 44.8 us
  Pallas kernels  43 us (96%)
  local copies, waits for them, and re-layouts  1.8 us (4%)
    pallas_call x1, Pallas kernels, shards(): pl.pallas_call(kernel, out_shape=jax.ShapeDtypeStruct((LOC, ROWS, I), F32...  43 us
    unnamed x1, local copies, waits for them, and re-layouts  1.8 us

profile of v2, /device:TPU:1, one launch (start us, length us, event | category | flops | bytes accessed | tf_op | source)
XLA Modules:
  0.0 44.8 jit_solution(9939678862401559851)
XLA Ops:
  0.0 43.0 %shard_map.91 = f32[3,23,1472]{2,1,0:T(8,128)} custom-call(f32[3,23,1472]{2,1,0:T(8,128)} %x_ref.1, f32[12,12]{1,0:T(8,128)} %to_ref.1, f32[12,12]{1,0:T(8,128)} %from_ref.1, f32[1,12]{1,0:T(1,128)} %bitcast.1, f32[8,1024]{1,0:T(8,128)} %constant.14.clone.line_ref, bf16[8,1536,256]{2,1,0:T(8,128)(2,1)} %constant.10.clone.fx_hbm, ...), custom_call_target="tpu_custom_call" | custom-call | flops 4000000000 | bytes 27000000 | tf_op jit(solution)/shard_map/pallas_call | solution.py:356
  43.0 1.8 %copy.11 = f32[3,23,1472]{2,1,0:T(8,128)} copy(f32[3,23,1472]{2,1,0:T(8,128)} %shard_map.91) | data formatting | bytes 812544

commit v3 on v2

--- a/solution.py
+++ b/solution.py
@@ -96,10 +96,10 @@
 
 
 def kernel(
-    x_ref, to_ref, from_ref, depth_ref, line_ref, fx_hbm, fy_hbm, iy_hbm, ix_hbm, out_ref,
-    fx, fy, iy, ix, xf, xs, ys, qs, ms, zs, part,
+    x_hbm, to_hbm, from_hbm, depth_hbm, line_hbm, fx_hbm, fy_hbm, iy_hbm, ix_hbm, out_hbm,
+    x_ref, to_ref, from_ref, depth_ref, line_ref, out_ref, fx, fy, iy, ix, xf, xs, ys, qs, ms, zs, part,
     swap_x, spec_x, send_a, recv_a, mid_a, mid_b, send_b, recv_b, home, other,
-    fx_sem, table_sem, swap_sem, s1_sem, s2_sem, r2_sem, s3_sem, r3_sem, all_sem,
+    in_sem, out_sem, fx_sem, table_sem, swap_sem, s1_sem, s2_sem, r2_sem, s3_sem, r3_sem, all_sem,
 ):
     wide = lax.axis_index("wide")
     lev = lax.axis_index("lev")
@@ -116,6 +116,17 @@
         return chip((q << 3) + ring)
 
     cross = me >> 3
+
+    small = [
+        pltpu.make_async_copy(source, target, in_sem.at[n])
+        for n, (source, target) in enumerate(
+            (
+                (x_hbm, x_ref), (to_hbm, to_ref), (from_hbm, from_ref),
+                (depth_hbm, depth_ref), (line_hbm, line_ref),
+            )
+        )
+    ]
+    small[0].start()
 
     blocks = [(core ^ 1) * COLS + c for c in range(COLS)] + [core * COLS + c for c in range(COLS)]
     fx_copies = []
@@ -140,10 +151,8 @@
         )
     pl.semaphore_signal(barrier, inc=1, device_id=partner, device_id_type=MESH)
 
-    for copy in rest:
-        copy.start()
-
     xf[...] = jnp.zeros_like(xf)
+    small[0].wait()
     for l in range(LOC):
         xf[l * PAD : l * PAD + ROWS, :I] = x_ref[l]
     high, low = split(xf[...])
@@ -166,16 +175,20 @@
         block = block.reshape(LOC, PAD, 128)
         if n < COLS:
             swap_x[n] = block
-            if n == 0:
+            if n == COLS - 1:
                 pl.semaphore_wait(barrier, RING - 1 + 15 + 1)
+                for c in range(COLS):
+                    swap_copy(c).start()
                 for step in range(1, 16):
                     pl.semaphore_signal(
                         all_sem, inc=1, device_id=across((cross + step) & 15), device_id_type=MESH
                     )
-            swap_copy(n).start()
         else:
             for l in range(LOC):
                 spec_x[core * LOC + l, n - COLS] = block[l]
+
+    for copy in small[1:] + rest:
+        copy.start()
 
     def bulk(ref, sem):
         return pltpu.make_async_copy(ref, ref, sem)
@@ -197,7 +210,7 @@
 
     pack(lambda l: spec_x[l].reshape(96, 128), send_a)
 
-    def exchange(source, target, send_sem, recv_sem):
+    def exchange(source, target, send_sem, recv_sem, between=None):
         def copy(s):
             return pltpu.make_async_remote_copy(
                 src_ref=source.at[pl.ds(pl.multiple_of(s * 8, 8), LAST)],
@@ -208,9 +221,18 @@
                 device_id_type=MESH,
             )
 
-        @pl.loop(1, CHIPS)
+        for step in range(1, RING):
+            copy(me - ring + ((ring + step) & (RING - 1))).start()
+        for step in range(1, 16):
+            copy((((cross + step) & 15) << 3) + ring).start()
+        if between is not None:
+            between()
+
+        @pl.loop(1, 16)
         def _(step):
-            copy((me + step) & (CHIPS - 1)).start()
+            q = ((cross + step) & 15) << 3
+            for turn in range(1, RING):
+                copy(q + ((ring + turn) & (RING - 1))).start()
 
         own = pl.ds(pl.multiple_of(me * 8, 8), 8)
         target[own, :] = source[own, :]
@@ -218,8 +240,9 @@
     def arrived(buffer, sem):
         bulk(buffer.at[pl.ds(0, (CHIPS - 1) * LAST)], sem).wait()
 
-    pl.semaphore_wait(all_sem, 15)
-    exchange(send_a, recv_a, s2_sem, r2_sem)
+    exchange(
+        send_a, recv_a, s2_sem, r2_sem, between=lambda: pl.semaphore_wait(all_sem, 15)
+    )
 
     row = lax.broadcasted_iota(jnp.int32, (M, 1), 0)
     pick = ((row >> 2) == lax.broadcasted_iota(jnp.int32, (M, K), 1)).astype(F32)
@@ -241,6 +264,8 @@
         low = full - high - middle
         return jnp.where(lane < 3 * M, high, jnp.where(lane < 5 * M, middle, low)).astype(BF16)
 
+    for copy in small[1:]:
+        copy.wait()
     to_big = expand(to_ref[...])
     from_big = expand(from_ref[...])
     depth = jnp.sum(pick * depth_ref[...], axis=1, keepdims=True)
@@ -250,11 +275,10 @@
     mag_q = jnp.sum(jnp.where(hit, line_ref[1:2], 0.0), axis=1, keepdims=True)
     left = lax.broadcasted_iota(jnp.int32, (M // 2, 128), 1) < WIDE
 
-    def mix(matrix, value):
+    def triple(value, lanes):
         high, middle, low = split_three(value)
         for n, piece in enumerate((high, middle, low, high, middle, high)):
-            qs[n * M : (n + 1) * M] = piece
-        return jnp.dot(matrix, qs[...], preferred_element_type=F32)
+            qs[n * M : (n + 1) * M, lanes] = piece
 
     arrived(recv_a, r2_sem)
 
@@ -273,24 +297,17 @@
 
     rest[0].wait()
 
-    @pl.loop(0, W // 256)
-    def _(j):
-        lanes = pl.ds(pl.multiple_of(j * 256, 256), 256)
-        spectrum = jnp.concatenate(
-            [
-                total(jnp.dot(ys[...], fy[2 * j + n], preferred_element_type=F32), M)
-                for n in range(2)
-            ],
-            axis=1,
-        )
-        modes = mix(to_big, spectrum)
-        lap_p = line_ref[0:1, lanes]
-        mag_p = line_ref[1:2, lanes]
-        keep = (mag_p * mag_p + mag_q * mag_q < float(KT * KT)).astype(F32)
-        solved = modes * keep / (1.0 + depth * (lap_p + lap_q))
-        high, low = split(mix(from_big, solved))
-        ms[:M, lanes] = high
-        ms[M:, lanes] = low
+    for j in range(W // 128):
+        lanes = slice(j * 128, j * 128 + 128)
+        triple(total(jnp.dot(ys[...], fy[j], preferred_element_type=F32), M), lanes)
+    lap_p = line_ref[0:1]
+    mag_p = line_ref[1:2]
+    keep = (mag_p * mag_p + mag_q * mag_q < float(KT * KT)).astype(F32)
+    modes = jnp.dot(to_big, qs[...], preferred_element_type=F32)
+    triple(modes * keep / (1.0 + depth * (lap_p + lap_q)), slice(0, W))
+    high, low = split(jnp.dot(from_big, qs[...], preferred_element_type=F32))
+    ms[:M] = high
+    ms[M:] = low
 
     rest[1].wait()
     for t in range(PAD // 2):
@@ -335,13 +352,23 @@
         )
     back.wait_recv()
     gather(lambda l: other[l])
+    leaving = []
     for j in range(N // 128):
         field = total(jnp.dot(zs[...], ix[core ^ 1, j], preferred_element_type=F32), 80)
         field = field + part[:, j * 128 : j * 128 + 128]
         width = min(128, I - j * 128)
         for l in range(LOC):
             out_ref[l, :, j * 128 : j * 128 + width] = field[l * PAD : l * PAD + ROWS, :width]
-
+        if j % 3 == 2:
+            lanes = slice((j - 2) * 128, j * 128 + width)
+            copy = pltpu.make_async_copy(
+                out_ref.at[:, :, lanes], out_hbm.at[:, :, lanes], out_sem.at[j // 3]
+            )
+            copy.start()
+            leaving.append(copy)
+
+    for copy in leaving:
+        copy.wait()
     bulk(swap_x, s1_sem).wait()
     arrived(send_a, s2_sem)
     arrived(send_b, s3_sem)
@@ -350,15 +377,20 @@
 
 def shards(state_field, to_modes, from_modes, mode_depth):
     fx, fy, iy, ix, line = (jnp.asarray(table) for table in tables())
-    vmem = pl.BlockSpec(memory_space=pltpu.VMEM)
     hbm = pl.BlockSpec(memory_space=pl.ANY)
     dma = pltpu.SemaphoreType.DMA
     return pl.pallas_call(
         kernel,
         out_shape=jax.ShapeDtypeStruct((LOC, ROWS, I), F32),
-        in_specs=[vmem] * 5 + [hbm] * 4,
-        out_specs=vmem,
+        in_specs=[hbm] * 9,
+        out_specs=hbm,
         scratch_shapes=[
+            pltpu.VMEM((LOC, ROWS, I), F32),
+            pltpu.VMEM((K, K), F32),
+            pltpu.VMEM((K, K), F32),
+            pltpu.VMEM((1, K), F32),
+            pltpu.VMEM(line.shape, F32),
+            pltpu.VMEM((LOC, ROWS, I), F32),
             pltpu.VMEM(fx.shape, BF16),
             pltpu.VMEM(fy.shape, BF16),
             pltpu.VMEM(iy.shape, BF16),
@@ -366,7 +398,7 @@
             pltpu.VMEM((80, N), F32),
             pltpu.VMEM((160, N), BF16),
             pltpu.VMEM((2 * M, N), BF16),
-            pltpu.VMEM((6 * M, 256), BF16),
+            pltpu.VMEM((6 * M, W), BF16),
             pltpu.VMEM((2 * M, W), BF16),
             pltpu.VMEM((160, W // 2), BF16),
             pltpu.VMEM((80, N), F32),
@@ -380,6 +412,8 @@
             pltpu.VMEM((8 * CHIPS, 128), F32),
             pltpu.VMEM((2 * LOC, 96, 128), F32),
             pltpu.VMEM((LOC, 96, 128), F32),
+            dma((5,)),
+            dma((4,)),
             dma((2 * COLS,)),
             dma((5,)),
             dma,

time: 45 us -> 43 us (0.956)
  Pallas kernels: 43 us -> 41.1 us
    pallas_call x1, Pallas kernels: 43 us -> 41.1 us  [shards(): pl.pallas_call(kernel, out_shape=jax.ShapeDtypeStruct((LOC, ROWS, I), F32...]
where the time goes in v3:
time: 43 us; the launch traced here: 42.9 us
  Pallas kernels  41.1 us (96%)
  local copies, waits for them, and re-layouts  1.8 us (4%)
    pallas_call x1, Pallas kernels, shards(): pl.pallas_call(kernel, out_shape=jax.ShapeDtypeStruct((LOC, ROWS, I), F32...  41.1 us
    unnamed x1, local copies, waits for them, and re-layouts  1.8 us

profile of v3, /device:TPU:1, one launch (start us, length us, event | category | flops | bytes accessed | tf_op | source)
XLA Modules:
  0.0 42.9 jit_solution(10487606468701878552)
XLA Ops:
  0.0 41.1 %shard_map.91 = f32[3,23,1472]{2,1,0:T(8,128)} custom-call(f32[3,23,1472]{2,1,0:T(8,128)} %x_hbm.1, f32[12,12]{1,0:T(8,128)} %to_hbm.1, f32[12,12]{1,0:T(8,128)} %from_hbm.1, f32[1,12]{1,0:T(1,128)} %bitcast.1, f32[8,1024]{1,0:T(8,128)} %constant.14.clone.line_hbm, bf16[8,1536,256]{2,1,0:T(8,128)(2,1)} %constant.10.clone.fx_hbm, ...), custom_call_target="tpu_custom_call" | custom-call | flops 4000000000 | bytes 27000000 | tf_op jit(solution)/shard_map/pallas_call | solution.py:382
  41.1 1.8 %copy.11 = f32[3,23,1472]{2,1,0:T(8,128)} copy(f32[3,23,1472]{2,1,0:T(8,128)} %shard_map.91) | data formatting | bytes 812544

commit v4 on v3

--- a/solution.py
+++ b/solution.py
@@ -96,10 +96,10 @@
 
 
 def kernel(
-    x_hbm, to_hbm, from_hbm, depth_hbm, line_hbm, fx_hbm, fy_hbm, iy_hbm, ix_hbm, out_hbm,
-    x_ref, to_ref, from_ref, depth_ref, line_ref, out_ref, fx, fy, iy, ix, xf, xs, ys, qs, ms, zs, part,
+    x_hbm, to_hbm, from_hbm, depth_hbm, line_hbm, fx_hbm, fy_hbm, iy_hbm, ix_hbm, out_ref,
+    x_ref, to_ref, from_ref, depth_ref, line_ref, fx, fy, iy, ix, xf, xs, ys, qs, ms, zs, part,
     swap_x, spec_x, send_a, recv_a, mid_a, mid_b, send_b, recv_b, home, other,
-    in_sem, out_sem, fx_sem, table_sem, swap_sem, s1_sem, s2_sem, r2_sem, s3_sem, r3_sem, all_sem,
+    in_sem, fx_sem, table_sem, swap_sem, s1_sem, s2_sem, r2_sem, s3_sem, r3_sem, all_sem,
 ):
     wide = lax.axis_index("wide")
     lev = lax.axis_index("lev")
@@ -352,23 +352,13 @@
         )
     back.wait_recv()
     gather(lambda l: other[l])
-    leaving = []
     for j in range(N // 128):
         field = total(jnp.dot(zs[...], ix[core ^ 1, j], preferred_element_type=F32), 80)
         field = field + part[:, j * 128 : j * 128 + 128]
         width = min(128, I - j * 128)
         for l in range(LOC):
             out_ref[l, :, j * 128 : j * 128 + width] = field[l * PAD : l * PAD + ROWS, :width]
-        if j % 3 == 2:
-            lanes = slice((j - 2) * 128, j * 128 + width)
-            copy = pltpu.make_async_copy(
-                out_ref.at[:, :, lanes], out_hbm.at[:, :, lanes], out_sem.at[j // 3]
-            )
-            copy.start()
-            leaving.append(copy)
-
-    for copy in leaving:
-        copy.wait()
+
     bulk(swap_x, s1_sem).wait()
     arrived(send_a, s2_sem)
     arrived(send_b, s3_sem)
@@ -381,16 +371,15 @@
     dma = pltpu.SemaphoreType.DMA
     return pl.pallas_call(
         kernel,
-        out_shape=jax.ShapeDtypeStruct((LOC, ROWS, I), F32),
+        out_shape=pltpu.VMEM((LOC, ROWS, I), F32),
         in_specs=[hbm] * 9,
-        out_specs=hbm,
+        out_specs=pl.BlockSpec(memory_space=pltpu.VMEM),
         scratch_shapes=[
             pltpu.VMEM((LOC, ROWS, I), F32),
             pltpu.VMEM((K, K), F32),
             pltpu.VMEM((K, K), F32),
             pltpu.VMEM((1, K), F32),
             pltpu.VMEM(line.shape, F32),
-            pltpu.VMEM((LOC, ROWS, I), F32),
             pltpu.VMEM(fx.shape, BF16),
             pltpu.VMEM(fy.shape, BF16),
             pltpu.VMEM(iy.shape, BF16),
@@ -413,7 +402,6 @@
             pltpu.VMEM((2 * LOC, 96, 128), F32),
             pltpu.VMEM((LOC, 96, 128), F32),
             dma((5,)),
-            dma((4,)),
             dma((2 * COLS,)),
             dma((5,)),
             dma,

time: 43 us -> 41.3 us (0.960)
  local copies, waits for them, and re-layouts: 1.8 us -> 0.76 us
  Pallas kernels: 41.1 us -> 40.4 us
    unnamed x1, local copies, waits for them, and re-layouts: 1.8 us -> 0.76 us
    pallas_call x1, Pallas kernels: 41.1 us -> 40.4 us  [shards(): pl.pallas_call(kernel, out_shape=pltpu.VMEM((LOC, ROWS, I), F32), in_spec...]
where the time goes in v4:
time: 41.3 us; the launch traced here: 41.2 us
  Pallas kernels  40.4 us (98%)
  local copies, waits for them, and re-layouts  0.76 us (2%)
    pallas_call x1, Pallas kernels, shards(): pl.pallas_call(kernel, out_shape=pltpu.VMEM((LOC, ROWS, I), F32), in_spec...  40.4 us

profile of v4, /device:TPU:1, one launch (start us, length us, event | category | flops | bytes accessed | tf_op | source)
XLA Modules:
  0.0 41.2 jit_solution(14703791425834528926)
XLA Ops:
  0.0 40.4 %shard_map.91 = f32[3,23,1472]{2,1,0:T(8,128)S(1)} custom-call(f32[3,23,1472]{2,1,0:T(8,128)} %x_hbm.1, f32[12,12]{1,0:T(8,128)} %to_hbm.1, f32[12,12]{1,0:T(8,128)} %from_hbm.1, f32[1,12]{1,0:T(1,128)} %bitcast.1, f32[8,1024]{1,0:T(8,128)} %constant.14.clone.line_hbm, bf16[8,1536,256]{2,1,0:T(8,128)(2,1)} %constant.10.clone.fx_hbm, ...), custom_call_target="tpu_custom_call" | custom-call | flops 4000000000 | bytes 27000000 | tf_op jit(solution)/shard_map/pallas_call | solution.py:372
  40.4 0.8 %copy.11 = f32[3,23,1472]{2,1,0:T(8,128)} copy(f32[3,23,1472]{2,1,0:T(8,128)S(1)} %shard_map.91) | data formatting | bytes 812544

commit v5 on v4

--- a/solution.py
+++ b/solution.py
@@ -175,14 +175,16 @@
         block = block.reshape(LOC, PAD, 128)
         if n < COLS:
             swap_x[n] = block
-            if n == COLS - 1:
+            if n == 0:
                 pl.semaphore_wait(barrier, RING - 1 + 15 + 1)
-                for c in range(COLS):
-                    swap_copy(c).start()
                 for step in range(1, 16):
                     pl.semaphore_signal(
                         all_sem, inc=1, device_id=across((cross + step) & 15), device_id_type=MESH
                     )
+                for c in range(n):
+                    swap_copy(c).start()
+            if n >= 0:
+                swap_copy(n).start()
         else:
             for l in range(LOC):
                 spec_x[core * LOC + l, n - COLS] = block[l]
@@ -221,18 +223,24 @@
                 device_id_type=MESH,
             )
 
-        for step in range(1, RING):
-            copy(me - ring + ((ring + step) & (RING - 1))).start()
-        for step in range(1, 16):
-            copy((((cross + step) & 15) << 3) + ring).start()
         if between is not None:
+            for step in range(1, RING):
+                copy(me - ring + ((ring + step) & (RING - 1))).start()
+            for step in range(1, 16):
+                copy((((cross + step) & 15) << 3) + ring).start()
             between()
 
-        @pl.loop(1, 16)
-        def _(step):
-            q = ((cross + step) & 15) << 3
-            for turn in range(1, RING):
-                copy(q + ((ring + turn) & (RING - 1))).start()
+            @pl.loop(1, 16)
+            def _(step):
+                q = ((cross + step) & 15) << 3
+                for turn in range(1, RING):
+                    copy(q + ((ring + turn) & (RING - 1))).start()
+
+        else:
+
+            @pl.loop(1, CHIPS)
+            def _(step):
+                copy((me + step) & (CHIPS - 1)).start()
 
         own = pl.ds(pl.multiple_of(me * 8, 8), 8)
         target[own, :] = source[own, :]

time: 41.3 us -> 40.8 us (0.988)
    pallas_call x1, Pallas kernels: 40.4 us -> 40 us  [shards(): pl.pallas_call(kernel, out_shape=pltpu.VMEM((LOC, ROWS, I), F32), in_spec...]
where the time goes in v5:
time: 40.8 us; the launch traced here: 40.7 us
  Pallas kernels  40 us (98%)
  local copies, waits for them, and re-layouts  0.76 us (2%)
    pallas_call x1, Pallas kernels, shards(): pl.pallas_call(kernel, out_shape=pltpu.VMEM((LOC, ROWS, I), F32), in_spec...  40 us

profile of v5, /device:TPU:1, one launch (start us, length us, event | category | flops | bytes accessed | tf_op | source)
XLA Modules:
  0.0 40.7 jit_solution(17717613096190075229)
XLA Ops:
  0.0 40.0 %shard_map.91 = f32[3,23,1472]{2,1,0:T(8,128)S(1)} custom-call(f32[3,23,1472]{2,1,0:T(8,128)} %x_hbm.1, f32[12,12]{1,0:T(8,128)} %to_hbm.1, f32[12,12]{1,0:T(8,128)} %from_hbm.1, f32[1,12]{1,0:T(1,128)} %bitcast.1, f32[8,1024]{1,0:T(8,128)} %constant.14.clone.line_hbm, bf16[8,1536,256]{2,1,0:T(8,128)(2,1)} %constant.10.clone.fx_hbm, ...), custom_call_target="tpu_custom_call" | custom-call | flops 4000000000 | bytes 27000000 | tf_op jit(solution)/shard_map/pallas_call | solution.py:380
  40.0 0.8 %copy.11 = f32[3,23,1472]{2,1,0:T(8,128)} copy(f32[3,23,1472]{2,1,0:T(8,128)S(1)} %shard_map.91) | data formatting | bytes 812544

commit v6 on v5

--- a/solution.py
+++ b/solution.py
@@ -82,6 +82,11 @@
     return high, (value - high.astype(F32)).astype(BF16)
 
 
+def stack(value):
+    high = value.astype(BF16).astype(F32)
+    return jnp.concatenate([high, value - high], axis=0).astype(BF16)
+
+
 def total(product, rows):
     return (
         (product[rows:, 128:] + product[:rows, 128:]) + product[rows:, :128]
@@ -155,9 +160,7 @@
     small[0].wait()
     for l in range(LOC):
         xf[l * PAD : l * PAD + ROWS, :I] = x_ref[l]
-    high, low = split(xf[...])
-    xs[:80] = high
-    xs[80:] = low
+    xs[...] = stack(xf[...])
 
     def swap_copy(c):
         return pltpu.make_async_remote_copy(
@@ -171,7 +174,7 @@
 
     for n in range(2 * COLS):
         fx_copies[n].wait()
-        block = total(jnp.dot(xs[...], fx[n], preferred_element_type=F32), 80)[: LOC * PAD]
+        block = total(jnp.dot(xs[...], fx[n], preferred_element_type=F32), LOC * PAD)
         block = block.reshape(LOC, PAD, 128)
         if n < COLS:
             swap_x[n] = block
@@ -224,23 +227,11 @@
             )
 
         if between is not None:
-            for step in range(1, RING):
-                copy(me - ring + ((ring + step) & (RING - 1))).start()
-            for step in range(1, 16):
-                copy((((cross + step) & 15) << 3) + ring).start()
             between()
 
-            @pl.loop(1, 16)
-            def _(step):
-                q = ((cross + step) & 15) << 3
-                for turn in range(1, RING):
-                    copy(q + ((ring + turn) & (RING - 1))).start()
-
-        else:
-
-            @pl.loop(1, CHIPS)
-            def _(step):
-                copy((me + step) & (CHIPS - 1)).start()
+        @pl.loop(1, CHIPS)
+        def _(step):
+            copy((me + step) & (CHIPS - 1)).start()
 
         own = pl.ds(pl.multiple_of(me * 8, 8), 8)
         target[own, :] = source[own, :]
@@ -349,19 +340,17 @@
     def gather(level):
         for c in range(COLS):
             rows = [level(l)[PAD * c : PAD * c + PAD] for l in range(LOC)]
-            high, low = split(jnp.concatenate(rows + [jnp.zeros((8, 128), F32)], axis=0))
-            zs[:80, c * 128 : c * 128 + 128] = high
-            zs[80:, c * 128 : c * 128 + 128] = low
+            zs[:, c * 128 : c * 128 + 128] = stack(jnp.concatenate(rows, axis=0))
 
     gather(lambda l: home[core * LOC + l])
     for j in range(N // 128):
         part[:, j * 128 : j * 128 + 128] = total(
-            jnp.dot(zs[...], ix[core, j], preferred_element_type=F32), 80
+            jnp.dot(zs[...], ix[core, j], preferred_element_type=F32), LOC * PAD
         )
     back.wait_recv()
     gather(lambda l: other[l])
     for j in range(N // 128):
-        field = total(jnp.dot(zs[...], ix[core ^ 1, j], preferred_element_type=F32), 80)
+        field = total(jnp.dot(zs[...], ix[core ^ 1, j], preferred_element_type=F32), LOC * PAD)
         field = field + part[:, j * 128 : j * 128 + 128]
         width = min(128, I - j * 128)
         for l in range(LOC):
@@ -392,13 +381,13 @@
             pltpu.VMEM(fy.shape, BF16),
             pltpu.VMEM(iy.shape, BF16),
             pltpu.VMEM(ix.shape, BF16),
-            pltpu.VMEM((80, N), F32),
-            pltpu.VMEM((160, N), BF16),
+            pltpu.VMEM((LOC * PAD, N), F32),
+            pltpu.VMEM((2 * LOC * PAD, N), BF16),
             pltpu.VMEM((2 * M, N), BF16),
             pltpu.VMEM((6 * M, W), BF16),
             pltpu.VMEM((2 * M, W), BF16),
-            pltpu.VMEM((160, W // 2), BF16),
-            pltpu.VMEM((80, N), F32),
+            pltpu.VMEM((2 * LOC * PAD, W // 2), BF16),
+            pltpu.VMEM((LOC * PAD, N), F32),
             pltpu.VMEM((COLS, LOC, PAD, 128), F32),
             pltpu.VMEM((2 * LOC, COLS, PAD, 128), F32),
             pltpu.VMEM((8 * CHIPS, 128), F32),

time: 40.8 us -> 40.5 us (level)
  no operation moved by 1% of the time
where the time goes in v6:
time: 40.5 us; the launch traced here: 40.4 us
  Pallas kernels  39.6 us (98%)
  local copies, waits for them, and re-layouts  0.76 us (2%)
    pallas_call x1, Pallas kernels, shards(): pl.pallas_call(kernel, out_shape=pltpu.VMEM((LOC, ROWS, I), F32), in_spec...  39.6 us

profile of v6, /device:TPU:1, one launch (start us, length us, event | category | flops | bytes accessed | tf_op | source)
XLA Modules:
  0.0 40.4 jit_solution(5613739838101545340)
XLA Ops:
  0.0 39.6 %shard_map.91 = f32[3,23,1472]{2,1,0:T(8,128)S(1)} custom-call(f32[3,23,1472]{2,1,0:T(8,128)} %x_hbm.1, f32[12,12]{1,0:T(8,128)} %to_hbm.1, f32[12,12]{1,0:T(8,128)} %from_hbm.1, f32[1,12]{1,0:T(1,128)} %bitcast.1, f32[8,1024]{1,0:T(8,128)} %constant.14.clone.line_hbm, bf16[8,1536,256]{2,1,0:T(8,128)(2,1)} %constant.10.clone.fx_hbm, ...), custom_call_target="tpu_custom_call" | custom-call | flops 4000000000 | bytes 27000000 | tf_op jit(solution)/shard_map/pallas_call | solution.py:369
  39.6 0.8 %copy.11 = f32[3,23,1472]{2,1,0:T(8,128)} copy(f32[3,23,1472]{2,1,0:T(8,128)S(1)} %shard_map.91) | data formatting | bytes 812544
